TPU v7x, 32 devices: a whole 2x2x4 slice. The times are simulated.
32 devices in a mesh: fsdp: 8 (over z, y), seq: 4 (over x, core).
Axes of the slice: x: 2, y: 2, z: 4, core: 2. Of those that a mesh axis runs over, the one named last changes fastest.
Arguments:
- draft_tokens: bfloat16 [8192, 2048], P('fsdp'), may hold values from -6 to 6
- draft_gate: bfloat16 [2048, 4096], P('fsdp', 'seq'), may hold values from -0.125 to 0.125
- draft_up: bfloat16 [2048, 4096], P('fsdp', 'seq'), may hold values from -0.125 to 0.125
- draft_head: float32 [4096], P('seq'), may hold values from -0.75 to 0.75
- verifier_rows: bfloat16 [8192, 8192], P(('fsdp', 'seq')), may hold values from -6 to 6
- norm_gain: float32 [8192], replicated, may hold values from 0.5 to 1.5
- key_weight: bfloat16 [8192, 512], P('fsdp'), may hold values from -0.06629126 to 0.06629126
- value_weight: bfloat16 [8192, 512], P('fsdp'), may hold values from -0.0625 to 0.0625
- pool_query: float32 [4, 4, 128], replicated, may hold values from -32 to 32
- flags: int32 [256], P(('fsdp', 'seq')), may hold values from 0 to 1, as said below
- owner: int32 [256], P(('fsdp', 'seq')), may hold values from 0 to 3
Outputs:
- draft_score: float32 [256], P(('fsdp', 'seq'))
- verdict: bfloat16 [256, 512], P(('fsdp', 'seq'))
Inputs may be any that keep to these rules, and one draw needn't show every extreme that they name: `flags`: on the 8 segments of one device, at most 4 flagged segments share an owner lane, and on every device exactly 4 flagged segments share one lane.
All inputs are finite; a program needn't handle non-finite values.
Results may differ from a plain program's by a relative error of at most 0.009.
Values may be sent and summed in bfloat16 or wider, within the bound.
A program may use at most 128 MiB of HBM per device.

v0:
```python
import math

import jax
import jax.numpy as jnp
from jax import lax
from jax.sharding import PartitionSpec as P

KVH = 4
HD = 128
SEGL = 32


eps = 1e-05


def normalize_rows(rows, norm_gain):
    values = rows.astype(jnp.float32)
    scale = lax.rsqrt(jnp.mean(values * values, axis=-1, keepdims=True) + eps)
    return (values * scale * norm_gain).astype(jnp.bfloat16)


def segment_pool(seg_keys, seg_values, queries, head_size):
    scores = jnp.einsum(
        "sthd,shd->sth", seg_keys, queries, precision=lax.Precision.HIGHEST
    ) / math.sqrt(head_size)
    scores = scores - jnp.max(scores, axis=1, keepdims=True)
    weights = jnp.exp(scores)
    weights = weights / jnp.sum(weights, axis=1, keepdims=True)
    summary_key = jnp.einsum("sth,sthd->shd", weights, seg_keys, precision=lax.Precision.HIGHEST)
    summary_value = jnp.einsum(
        "sth,sthd->shd", weights, seg_values, precision=lax.Precision.HIGHEST
    )
    return (summary_key, summary_value)


def cross_pool(query_keys, key_all, value_all, live_all, head_size):
    scores = jnp.einsum(
        "jhd,ihd->jhi", query_keys, key_all, precision=lax.Precision.HIGHEST
    ) / math.sqrt(head_size)
    scores = jnp.where(live_all[None, None, :], scores, -1e30)
    highest = jnp.max(scores, axis=2, keepdims=True)
    weights = jnp.where(live_all[None, None, :], jnp.exp(scores - highest), 0.0)
    total = jnp.sum(weights, axis=2, keepdims=True)
    return jnp.einsum("jhi,ihd->jhd", weights, value_all, precision=lax.Precision.HIGHEST) / total


def project_pair(row_block, pieces):
    return (
        jnp.dot(row_block, pieces[0], preferred_element_type=jnp.float32),
        jnp.dot(row_block, pieces[1], preferred_element_type=jnp.float32),
    )


def local(
    draft_tokens,
    draft_gate,
    draft_up,
    draft_head,
    verifier_rows,
    norm_gain,
    key_weight,
    value_weight,
    pool_query,
    flags,
    owner,
):
    seg_count = flags.shape[0]
    gate, upward = project_pair(
        draft_tokens,
        (
            lax.all_gather(draft_gate, "fsdp", axis=0, tiled=True),
            lax.all_gather(draft_up, "fsdp", axis=0, tiled=True),
        ),
    )
    partial_scores = jnp.sum(jax.nn.silu(gate) * upward * draft_head[None, :], axis=1)
    own_scores = lax.psum_scatter(partial_scores, "seq", scatter_dimension=0, tiled=True)
    draft_score = jnp.mean(own_scores.reshape(seg_count, SEGL), axis=1)
    normed = normalize_rows(verifier_rows, norm_gain)
    seg_keys, seg_values = project_pair(
        normed,
        (
            lax.all_gather(key_weight, "fsdp", axis=0, tiled=True),
            lax.all_gather(value_weight, "fsdp", axis=0, tiled=True),
        ),
    )
    lane_pick = (
        owner[:, None] == jnp.arange(pool_query.shape[0], dtype=jnp.int32)[None, :]
    ).astype(jnp.float32)
    queries = jnp.einsum("sc,chd->shd", lane_pick, pool_query, precision=lax.Precision.HIGHEST)
    summary_key, summary_value = segment_pool(
        seg_keys.reshape(seg_count, SEGL, KVH, HD),
        seg_values.reshape(seg_count, SEGL, KVH, HD),
        queries,
        HD,
    )
    live_own = flags.astype(jnp.float32)
    key_all, value_all, live_all = (
        lax.all_gather(summary_key.reshape(seg_count, KVH * HD), "seq", axis=0, tiled=True),
        lax.all_gather(summary_value.reshape(seg_count, KVH * HD), "seq", axis=0, tiled=True),
        lax.all_gather(live_own, "seq", axis=0, tiled=True),
    )
    pooled = cross_pool(
        summary_key,
        key_all.reshape(-1, KVH, HD),
        value_all.reshape(-1, KVH, HD),
        live_all > 0.5,
        HD,
    )
    own_pooled = pooled.reshape(seg_count, KVH * HD)
    verdict = jnp.where(
        flags[:, None] == 1, jax.nn.sigmoid(draft_score)[:, None] * own_pooled, 0.0
    ).astype(jnp.bfloat16)
    return (draft_score, verdict)


def solution(mesh):
    return jax.shard_map(
        local,
        mesh=mesh,
        in_specs=(
            P("fsdp", None),
            P("fsdp", "seq"),
            P("fsdp", "seq"),
            P("seq"),
            P(("fsdp", "seq"), None),
            P(),
            P("fsdp", None),
            P("fsdp", None),
            P(),
            P(("fsdp", "seq")),
            P(("fsdp", "seq")),
        ),
        out_specs=(P(("fsdp", "seq")), P(("fsdp", "seq"), None)),
        check_vma=False,
    )
```

profile of v0, /device:TPU:0, one launch (start us, length us, event | category | flops | bytes accessed | tf_op | source)
XLA Modules:
  0.0 431.5 jit_solution(6430175980081198949)
XLA Ops:
  7.2 0.0 copy-start
  7.2 0.0 all-gather.5.cloned.1.call-start
  7.2 0.7 all-gather.5.cloned.1.call-update
  7.9 0.0 all-gather.7.cloned.1.call-start
  8.0 0.7 all-gather.7.cloned.1.call-update
  8.7 0.0 all-gather.9.cloned.1.call-start
  8.7 0.7 all-gather.9.cloned.1.call-update
  9.4 0.0 all-gather.11.cloned.1.call-start
  9.4 0.5 all-gather.11.cloned.1.call-update
  10.0 1.3 fusion.44
  12.6 0.0 copy-done
  12.6 0.9 convolution_bitcast_fusion.1
  13.5 0.7 broadcast_compare_fusion.1
  14.1 0.7 convert_dynamic-update-slice_fusion
  14.9 3.1 fusion.1
  18.0 0.0 copy-start.2
  18.0 68.3 %all-gather.5.cloned.1.call-done = bf16[2048,1024]{1,0:T(8,128)(2,1)} async-done(((bf16[256,1024]{1,0:T(8,128)(2,1)}), bf16[2048,1024]{1,0:T(8,128)(2,1)}) %all-gather.5.cloned.1.call-update) | async-done | bytes 4194320 | tf_op jit(solution)/shard_map/all_gather | solution.py:71
  86.3 10.0 %fusion.47 = f32[1024,1024]{0,1:T(8,128)} fusion(bf16[1024,2048]{1,0:T(8,128)(2,1)} %param.11, bf16[2048,1024]{1,0:T(8,128)(2,1)} %all-gather.5.cloned.1.call-done), kind=kOutput, calls=%fused_computation.63 | convolution fusion | flops 4294967296 | bytes 12582912 | tf_op jit(solution)/shard_map/dot_general | solution.py:49
  96.3 0.0 copy-start.1
  96.3 63.8 %all-gather.7.cloned.1.call-done = bf16[2048,1024]{1,0:T(8,128)(2,1)} async-done(((bf16[256,1024]{1,0:T(8,128)(2,1)}), bf16[2048,1024]{1,0:T(8,128)(2,1)}) %all-gather.7.cloned.1.call-update) | async-done | bytes 4194320 | tf_op jit(solution)/shard_map/all_gather | solution.py:72
  160.1 0.0 copy-done.2
  160.1 10.1 %multiply_reduce_fusion = f32[1024]{0:T(1024)S(1)} fusion(f32[1024,1024]{0,1:T(8,128)} %fusion.47, bf16[1024,2048]{1,0:T(8,128)(2,1)} %param.11, bf16[2048,1024]{1,0:T(8,128)(2,1)} %all-gather.7.cloned.1.call-done, f32[1024]{0:T(1024)S(1)} %copy-done.2), kind=kOutput, calls=%fused_computation.6 | convolution fusion | flops 4302306304 | bytes 12591104 | tf_op jit(solution)/shard_map/dot_general | solution.py:50
  170.2 6.3 %all-reduce.2 = (f32[1024]{0:T(1024)S(1)}, f32[32]{0:T(128)S(1)}) all-reduce(f32[1024]{0:T(1024)S(1)} %multiply_reduce_fusion, f32[32]{0:T(128)S(1)} %convert_dynamic-update-slice_fusion), channel_id=2, replica_groups=mesh['fsdp'=8,'seq'=4] {'seq'}, use_global_device_ids=true, to_apply=%region_1.2.clone | all-reduce | flops 1056 | bytes 8448
  176.6 0.1 dynamic-slice.2
  176.7 0.1 reshape.53
  176.7 0.1 reduce_sum.46
  176.9 0.5 add_divide_fusion
  177.4 108.1 %all-gather.9.cloned.1.call-done = bf16[8192,512]{1,0:T(8,128)(2,1)} async-done(((bf16[1024,512]{1,0:T(8,128)(2,1)}), bf16[8192,512]{1,0:T(8,128)(2,1)}) %all-gather.9.cloned.1.call-update) | async-done | bytes 8388624 | tf_op jit(solution)/shard_map/all_gather | solution.py:82
  285.5 0.0 copy-done.1
  285.5 7.0 %fusion.6 = f32[256,512]{1,0:T(8,128)S(1)} fusion(bf16[8192,512]{1,0:T(8,128)(2,1)} %all-gather.9.cloned.1.call-done, bf16[256,8192]{1,0:T(8,128)(2,1)} %param.15, f32[8192]{0:T(1024)S(1)} %copy-done.1, f32[256]{0:T(256)S(1)} %add_rsqrt_fusion), kind=kOutput, calls=%fused_computation.8 | convolution fusion | flops 2155872256 | bytes 13140992 | tf_op jit(solution)/shard_map/dot_general | solution.py:49
  292.5 0.2 reshape.54
  292.7 0.9 fusion.21
  293.6 0.7 fusion.45
  294.3 0.1 divide_bitcast_fusion
  294.4 0.6 fusion.19
  294.9 5.2 %all_gather.27 = f32[32,512]{1,0:T(8,128)S(1)} all-gather(f32[8,512]{1,0:T(8,128)S(1)} %bitcast.83), channel_id=1, replica_groups=mesh['fsdp'=8,'seq'=4] {'seq'}, dimensions={0}, use_global_device_ids=true | all-gather | bytes 81920 | tf_op jit(solution)/shard_map/all_gather | solution.py:98
  300.2 110.5 %all-gather.11.cloned.1.call-done = bf16[8192,512]{1,0:T(8,128)(2,1)} async-done(((bf16[1024,512]{1,0:T(8,128)(2,1)}), bf16[8192,512]{1,0:T(8,128)(2,1)}) %all-gather.11.cloned.1.call-update) | async-done | bytes 8388624 | tf_op jit(solution)/shard_map/all_gather | solution.py:83
  410.7 7.0 %fusion.4 = f32[256,512]{1,0:T(8,128)S(1)} fusion(bf16[8192,512]{1,0:T(8,128)(2,1)} %all-gather.11.cloned.1.call-done, bf16[256,8192]{1,0:T(8,128)(2,1)} %param.15, f32[8192]{0:T(1024)S(1)} %copy-done.1, f32[256]{0:T(256)S(1)} %add_rsqrt_fusion), kind=kOutput, calls=%fused_computation.7 | convolution fusion | flops 2155872256 | bytes 13140992 | tf_op jit(solution)/shard_map/dot_general | solution.py:50
  417.7 0.2 reshape.55
  417.9 0.5 fusion.17
  418.4 5.2 %all_gather.25 = f32[32,512]{1,0:T(8,128)S(1)} all-gather(f32[8,512]{1,0:T(8,128)S(1)} %bitcast.82), channel_id=1, replica_groups=mesh['fsdp'=8,'seq'=4] {'seq'}, dimensions={0}, use_global_device_ids=true | all-gather | bytes 81920 | tf_op jit(solution)/shard_map/all_gather | solution.py:99
  423.7 0.3 fusion.46
  424.0 0.2 fusion.31
  424.1 0.9 fusion.16
  (5 shorter events, 0.0 us)
Async XLA Ops:
  7.2 5.4 %copy-start = (f32[4,4,128]{2,1,0:T(4,128)S(1)}, f32[4,4,128]{2,1,0:T(4,128)}, u32[]{:S(2)}) copy-start(f32[4,4,128]{2,1,0:T(4,128)} %param.19) | copy-start | bytes 24580
  7.2 79.1 %all-gather.5.cloned.1.call-start = ((), (), s32[]{:S(2)}) async-start(), calls=%async_computation | async-start | bytes 4718592 | tf_op jit(solution)/shard_map/all_gather | solution.py:71
  7.9 152.2 %all-gather.7.cloned.1.call-start = ((), (), s32[]{:S(2)}) async-start(), calls=%async_computation.1 | async-start | bytes 4718592 | tf_op jit(solution)/shard_map/all_gather | solution.py:72
  8.7 276.8 %all-gather.9.cloned.1.call-start = ((), (), s32[]{:S(2)}) async-start(), calls=%async_computation.2 | async-start | bytes 9437184 | tf_op jit(solution)/shard_map/all_gather | solution.py:82
  9.4 401.3 %all-gather.11.cloned.1.call-start = ((), (), s32[]{:S(2)}) async-start(), calls=%async_computation.3 | async-start | bytes 9437184 | tf_op jit(solution)/shard_map/all_gather | solution.py:83
  18.0 142.1 %copy-start.2 = (f32[1024]{0:T(1024)S(1)}, f32[1024]{0:T(1024)}, u32[]{:S(2)}) copy-start(f32[1024]{0:T(1024)} %param.14) | copy-start | bytes 12292
  96.3 189.2 %copy-start.1 = (f32[8192]{0:T(1024)S(1)}, f32[8192]{0:T(1024)}, u32[]{:S(2)}) copy-start(f32[8192]{0:T(1024)} %param.16) | copy-start | bytes 98308
Sparse Core Ops, SparseCore 0:
  10.1 76.0 all-gather.4
  88.4 71.6 all-gather.6
  162.2 123.1 all-gather.8
  287.4 123.1 all-gather.10
where the time goes:
time: 432 us
  waiting for transfers between devices  353 us (82%)
  matrix products  38.2 us (9%)
  blocking collectives  16.8 us (4%)
  between operations  15.2 us (4%)
  other arithmetic  6.08 us (1%)
    all_gather x1, waiting for transfers between devices, local(): lax.all_gather(value_weight, 'fsdp', axis=0, tiled=True)  110 us
    all_gather x1, waiting for transfers between devices, local(): lax.all_gather(key_weight, 'fsdp', axis=0, tiled=True)  108 us
    all_gather x1, waiting for transfers between devices, local(): lax.all_gather(draft_gate, 'fsdp', axis=0, tiled=True)  68.3 us
    all_gather x1, waiting for transfers between devices, local(): lax.all_gather(draft_up, 'fsdp', axis=0, tiled=True)  63.8 us
    dot_general x2, matrix products, project_pair(): jnp.dot(row_block, pieces[1], preferred_element_type=jnp.float32)  17.2 us
    dot_general x2, matrix products, project_pair(): jnp.dot(row_block, pieces[0], preferred_element_type=jnp.float32)  17 us
  transfers between devices with their start and end apart: 4, of which 4 were waited for; matrix products, arithmetic and copies ran while one was open for 9% of the time, Pallas kernels for 0%

commit v1 on v0

v1 whole, which is shorter than its diff:
```python
import functools
import math

import jax
import jax.numpy as jnp
from jax import lax
from jax.experimental import pallas as pl
from jax.experimental.pallas import tpu as pltpu
from jax.sharding import PartitionSpec as P

KVH = 4
HD = 128
SEGL = 32


eps = 1e-05


def normalize_rows(rows, norm_gain):
    values = rows.astype(jnp.float32)
    scale = lax.rsqrt(jnp.mean(values * values, axis=-1, keepdims=True) + eps)
    return (values * scale * norm_gain).astype(jnp.bfloat16)


def split_pair(values):
    high = lax.reduce_precision(values, 8, 7)
    return high.astype(jnp.bfloat16), (values - high).astype(jnp.bfloat16)


def pooled_summaries(normed, key_weight, value_weight, pool_query, owner):
    lanes = pool_query.shape[0]
    segs = owner.shape[0]
    groups = lax.axis_size("fsdp")
    depth = key_weight.shape[0]
    key_heads = key_weight.reshape(depth, KVH, HD)
    value_heads = value_weight.reshape(depth, KVH, HD)
    turned = jnp.einsum(
        "chk,dhk->chd",
        pool_query,
        key_heads.astype(jnp.float32),
        precision=lax.Precision.HIGHEST,
    ).reshape(lanes * KVH, depth) / math.sqrt(HD)
    turned = lax.all_gather(turned, "fsdp", axis=0)
    turned = turned.transpose(1, 0, 2).reshape(lanes * KVH, groups * depth)
    both = lax.dot_general(
        normed,
        jnp.concatenate(split_pair(turned), axis=0),
        (((1,), (1,)), ((), ())),
        preferred_element_type=jnp.float32,
    )
    scores = (both[:, : lanes * KVH] + both[:, lanes * KVH :]).reshape(segs, SEGL, lanes, KVH)
    pick = owner[:, None] == jnp.arange(lanes, dtype=jnp.int32)[None, :]
    scores = jnp.sum(jnp.where(pick[:, None, :, None], scores, 0.0), axis=2)
    scores = scores - jnp.max(scores, axis=1, keepdims=True)
    weights = jnp.exp(scores)
    weights = weights / jnp.sum(weights, axis=1, keepdims=True)
    spread = jnp.eye(segs, dtype=jnp.float32)[:, None, :, None] * jnp.transpose(
        weights, (2, 0, 1)
    ).transpose(1, 0, 2)[:, :, None, :]
    spread = spread.reshape(segs * KVH, segs * SEGL)
    high, low = split_pair(spread)
    pools = jnp.dot(jnp.concatenate([high, low], axis=0), normed, preferred_element_type=jnp.float32)
    pools = (pools[: segs * KVH] + pools[segs * KVH :]).astype(jnp.bfloat16)
    pools = pools.reshape(segs * KVH, groups, depth).transpose(1, 0, 2)
    pools = lax.all_to_all(pools, "fsdp", 0, 0).reshape(groups * segs, KVH, depth)
    partial = jnp.stack(
        [
            jnp.einsum("ghd,dhk->ghk", pools, heads, preferred_element_type=jnp.float32)
            for heads in (key_heads, value_heads)
        ]
    ).reshape(2, groups, segs, KVH * HD)
    partial = lax.all_to_all(partial.transpose(1, 0, 2, 3), "fsdp", 0, 0)
    summaries = jnp.sum(partial, axis=0).reshape(2, segs, KVH, HD)
    return summaries[0], summaries[1]


def cross_pool(query_keys, key_all, value_all, live_all, head_size):
    scores = jnp.einsum(
        "jhd,ihd->jhi", query_keys, key_all, precision=lax.Precision.HIGHEST
    ) / math.sqrt(head_size)
    scores = jnp.where(live_all[None, None, :], scores, -1e30)
    highest = jnp.max(scores, axis=2, keepdims=True)
    weights = jnp.where(live_all[None, None, :], jnp.exp(scores - highest), 0.0)
    total = jnp.sum(weights, axis=2, keepdims=True)
    return jnp.einsum("jhi,ihd->jhd", weights, value_all, precision=lax.Precision.HIGHEST) / total


def project_pair(row_block, pieces):
    return (
        jnp.dot(row_block, pieces[0], preferred_element_type=jnp.float32),
        jnp.dot(row_block, pieces[1], preferred_element_type=jnp.float32),
    )


def draft_gathered(draft_tokens, draft_gate, draft_up, draft_head, seg_count):
    gate, upward = project_pair(
        draft_tokens,
        (
            lax.all_gather(draft_gate, "fsdp", axis=0, tiled=True),
            lax.all_gather(draft_up, "fsdp", axis=0, tiled=True),
        ),
    )
    partial_scores = jnp.sum(jax.nn.silu(gate) * upward * draft_head[None, :], axis=1)
    own_scores = lax.psum_scatter(partial_scores, "seq", scatter_dimension=0, tiled=True)
    return jnp.mean(own_scores.reshape(seg_count, SEGL), axis=1)


DEPTHS = 4
WIDE = 512


def plane_kernel_body(
    tok_hbm, gate_hbm, up_hbm, head_ref, out_ref,
    tok, wg, wu, sums, gathered,
    tok_sem, first_send, near_send, far_send, arrive,
    tok_send, tok_arrive, sum_send, sum_arrive,
):
    f = lax.axis_index("fsdp")
    s = lax.axis_index("seq")
    z, y = f // 2, f % 2
    x, c = s // 2, s % 2
    weights = (wg, wu)
    rows = tok_hbm.shape[0]
    depth = gate_hbm.shape[0]
    mesh_id = pl.DeviceIdType.MESH

    barrier = pltpu.get_barrier_semaphore()
    peers = []
    for dy in range(2):
        for ds in range(4):
            if dy or ds:
                peers.append((dy, ds, 2 * z + lax.rem(y + dy, 2), lax.rem(s + ds, 4)))
    for _, _, pf, ps in peers:
        pl.semaphore_signal(barrier, inc=1, device_id=(pf, ps), device_id_type=mesh_id)

    @pl.when(z > 0)
    def _():
        pl.semaphore_signal(barrier, inc=1, device_id=(f - 2, s), device_id_type=mesh_id)

    @pl.when(z < DEPTHS - 1)
    def _():
        pl.semaphore_signal(barrier, inc=1, device_id=(f + 2, s), device_id_type=mesh_id)

    @pl.when(jnp.logical_or(z == 0, z == DEPTHS - 1))
    def _():
        pl.semaphore_wait(barrier, 8)

    @pl.when(jnp.logical_and(z > 0, z < DEPTHS - 1))
    def _():
        pl.semaphore_wait(barrier, 9)

    def slot(ref, index):
        return ref.at[pl.ds(pl.multiple_of(index * depth, depth), depth), :]

    def first(half, part):
        source = (gate_hbm, up_hbm)[part].at[:, half * WIDE : (half + 1) * WIDE]
        return pltpu.make_async_remote_copy(
            src_ref=source,
            dst_ref=slot(weights[part], f),
            send_sem=first_send.at[half, part],
            recv_sem=arrive.at[f, part],
            device_id=(2 * z + c, 2 * x + half),
            device_id_type=mesh_id,
        )

    def kept(half, part):
        source = (gate_hbm, up_hbm)[part].at[:, half * WIDE : (half + 1) * WIDE]
        return pltpu.make_async_copy(source, slot(weights[part], f), arrive.at[f, part])

    def is_self(half):
        return jnp.logical_and(c == y, c == half)

    for half in range(2):
        @pl.when(jnp.logical_not(is_self(half)))
        def _():
            for part in range(2):
                first(half, part).start()

        @pl.when(is_self(half))
        def _():
            for part in range(2):
                kept(half, part).start()

    other_f = 2 * z + 1 - y
    chunks = 4
    size = rows // 2 // chunks

    def chunk_rows(core, chunk):
        return pl.multiple_of(core * (rows // 2) + chunk * size, size)

    def tok_across(chunk):
        start = chunk_rows(c, chunk)
        return pltpu.make_async_remote_copy(
            src_ref=tok_hbm.at[pl.ds(start, size), :],
            dst_ref=tok.at[pl.ds(rows + start, size), :],
            send_sem=tok_send.at[0, chunk],
            recv_sem=tok_arrive.at[0, chunk],
            device_id=(other_f, s),
            device_id_type=mesh_id,
        )

    def tok_over(chunk):
        start = rows + chunk_rows(c, chunk)
        return pltpu.make_async_remote_copy(
            src_ref=tok.at[pl.ds(start, size), :],
            dst_ref=tok.at[pl.ds(start, size), :],
            send_sem=tok_send.at[1, chunk],
            recv_sem=tok_arrive.at[1, chunk],
            device_id=(f, 2 * x + 1 - c),
            device_id_type=mesh_id,
        )

    for chunk in range(chunks):
        tok_across(chunk).start()
    own_tokens = pltpu.make_async_copy(tok_hbm, tok.at[pl.ds(0, rows), :], tok_sem)
    own_tokens.start()

    def forward(index, part, step):
        sems = near_send if step < 0 else far_send
        return pltpu.make_async_remote_copy(
            src_ref=slot(weights[part], index),
            dst_ref=slot(weights[part], index),
            send_sem=sems.at[index, part],
            recv_sem=arrive.at[index, part],
            device_id=(f + 2 * step, s),
            device_id_type=mesh_id,
        )

    def arrived(index):
        for part in range(2):
            forward(index, part, 1).wait_recv()

    def both(index, step, wait):
        for part in range(2):
            if wait:
                forward(index, part, step).wait_send()
            else:
                forward(index, part, step).start()

    def turn(distance, flip, wait):
        side = y if flip == 0 else 1 - y
        if distance == 0:
            index = f if flip == 0 else other_f
            if not wait:
                arrived(index)

            @pl.when(z < DEPTHS - 1)
            def _():
                both(index, 1, wait)

            @pl.when(z > 0)
            def _():
                both(index, -1, wait)

            return

        @pl.when(z >= distance)
        def _():
            index = 2 * (z - distance) + side
            if not wait:
                arrived(index)

            @pl.when(z < DEPTHS - 1)
            def _():
                both(index, 1, wait)

        @pl.when(z + distance < DEPTHS)
        def _():
            index = 2 * (z + distance) + side
            if not wait:
                arrived(index)

            @pl.when(z > 0)
            def _():
                both(index, -1, wait)

    order = ((0, 0), (1, 0), (0, 1), (2, 0), (1, 1), (3, 0), (2, 1), (3, 1))
    passed = 0
    for number, (distance, flip) in enumerate(order):
        turn(distance, flip, False)
        if number >= 2 and passed < chunks:
            tok_across(passed).wait_recv()
            tok_over(passed).start()
            passed += 1
    for chunk in range(chunks):
        tok_over(chunk).wait_recv()
    own_tokens.wait()

    tile = 512
    per = rows // 4
    head = head_ref[...]

    @pl.loop(0, 2 * rows // tile)
    def _(step):
        block = tok[pl.ds(pl.multiple_of(step * tile, tile), tile), :]
        gate = jnp.dot(block, wg[...], preferred_element_type=jnp.float32)
        upward = jnp.dot(block, wu[...], preferred_element_type=jnp.float32)
        product = gate / (1.0 + jnp.exp(-gate)) * upward * head
        by_seg = jnp.sum(product.reshape(tile // SEGL, SEGL, WIDE), axis=1)
        lanes = by_seg[:, 0:128]
        for lane in range(1, WIDE // 128):
            lanes = lanes + by_seg[:, lane * 128 : (lane + 1) * 128]
        for piece in range(tile // per):
            sums[(tile // per) * step + piece] = lanes[piece * 8 : (piece + 1) * 8, :]

    def sum_copy(number, dy, pf, ps):
        return pltpu.make_async_remote_copy(
            src_ref=sums.at[4 * dy + ps],
            dst_ref=gathered.at[number],
            send_sem=sum_send.at[number],
            recv_sem=sum_arrive.at[number],
            device_id=(pf, ps),
            device_id_type=mesh_id,
        )

    for number, (dy, ds, pf, ps) in enumerate(peers):
        sum_copy(number, dy, pf, ps).start()
    total = sums[s]
    for number, (dy, ds, pf, ps) in enumerate(peers):
        sum_copy(number, dy, pf, ps).wait_recv()
        total = total + gathered[number]
    out_ref[...] = total

    for half in range(2):
        @pl.when(jnp.logical_not(is_self(half)))
        def _():
            for part in range(2):
                first(half, part).wait_send()
    for chunk in range(chunks):
        tok_across(chunk).wait_send()
        tok_over(chunk).wait_send()
    for distance, flip in order:
        turn(distance, flip, True)
    for number, (dy, ds, pf, ps) in enumerate(peers):
        sum_copy(number, dy, pf, ps).wait_send()


def draft_plane(draft_tokens, draft_gate, draft_up, draft_head):
    rows, width = draft_tokens.shape
    y = lax.axis_index("fsdp") % 2
    x, c = lax.axis_index("seq") // 2, lax.axis_index("seq") % 2
    every = lax.all_gather(draft_head, "seq", axis=0, tiled=True)
    head = lax.dynamic_slice(every, ((2 * x + y) * 2 * WIDE + c * WIDE,), (WIDE,))
    sems = pltpu.SemaphoreType.DMA
    tiles = pl.pallas_call(
        plane_kernel_body,
        out_shape=jax.ShapeDtypeStruct((8, 128), jnp.float32),
        in_specs=[pl.BlockSpec(memory_space=pl.ANY)] * 3
        + [pl.BlockSpec(memory_space=pltpu.VMEM)],
        out_specs=pl.BlockSpec(memory_space=pltpu.VMEM),
        scratch_shapes=[
            pltpu.VMEM((2 * rows, width), jnp.bfloat16),
            pltpu.VMEM((width, WIDE), jnp.bfloat16),
            pltpu.VMEM((width, WIDE), jnp.bfloat16),
            pltpu.VMEM((8, 8, 128), jnp.float32),
            pltpu.VMEM((7, 8, 128), jnp.float32),
            sems,
            sems((2, 2)),
            sems((8, 2)),
            sems((8, 2)),
            sems((8, 2)),
            sems((2, 4)),
            sems((2, 4)),
            sems((7,)),
            sems((7,)),
        ],
        compiler_params=pltpu.CompilerParams(
            collective_id=0, has_side_effects=True, vmem_limit_bytes=40 * 1024 * 1024
        ),
        cost_estimate=pl.CostEstimate(
            flops=4 * 2 * rows * width * WIDE,
            bytes_accessed=24 * 1024 * 1024,
            transcendentals=2 * rows * WIDE,
        ),
    )(draft_tokens, draft_gate, draft_up, head[None, :])
    return jnp.sum(tiles, axis=1) / SEGL


def local(
    plane_kernel,
    draft_tokens,
    draft_gate,
    draft_up,
    draft_head,
    verifier_rows,
    norm_gain,
    key_weight,
    value_weight,
    pool_query,
    flags,
    owner,
):
    seg_count = flags.shape[0]
    if plane_kernel:
        draft_score = draft_plane(draft_tokens, draft_gate, draft_up, draft_head)
    else:
        draft_score = draft_gathered(draft_tokens, draft_gate, draft_up, draft_head, seg_count)
    normed = normalize_rows(verifier_rows, norm_gain)
    summary_key, summary_value = pooled_summaries(
        normed, key_weight, value_weight, pool_query, owner
    )
    live_own = flags.astype(jnp.float32)
    width = KVH * HD
    packed = jnp.concatenate(
        [
            summary_key.reshape(seg_count, width),
            summary_value.reshape(seg_count, width),
            jnp.broadcast_to(live_own[:, None], (seg_count, 128)),
        ],
        axis=1,
    )
    every = lax.all_gather(packed, "seq", axis=0, tiled=True)
    pooled = cross_pool(
        summary_key,
        every[:, :width].reshape(-1, KVH, HD),
        every[:, width : 2 * width].reshape(-1, KVH, HD),
        every[:, 2 * width] > 0.5,
        HD,
    )
    own_pooled = pooled.reshape(seg_count, KVH * HD)
    verdict = jnp.where(
        flags[:, None] == 1, jax.nn.sigmoid(draft_score)[:, None] * own_pooled, 0.0
    ).astype(jnp.bfloat16)
    return (draft_score, verdict)


def solution(mesh):
    plane_kernel = dict(mesh.shape) == {"fsdp": 2 * DEPTHS, "seq": 4}
    return jax.shard_map(
        functools.partial(local, plane_kernel),
        mesh=mesh,
        in_specs=(
            P("fsdp", None),
            P("fsdp", "seq"),
            P("fsdp", "seq"),
            P("seq"),
            P(("fsdp", "seq"), None),
            P(),
            P("fsdp", None),
            P("fsdp", None),
            P(),
            P(("fsdp", "seq")),
            P(("fsdp", "seq")),
        ),
        out_specs=(P(("fsdp", "seq")), P(("fsdp", "seq"), None)),
        check_vma=False,
    )
```

time: 432 us -> 169 us (0.39)
  waiting for transfers between devices: 353 us -> 5.02 us
  Pallas kernels: 0 us -> 88.4 us
  matrix products: 38.2 us -> 9.9 us
  blocking collectives: 16.8 us -> 43.8 us
  between operations: 15.2 us -> 0.9 us
  starting transfers between devices: 0.15 us -> 9.51 us
    all_gather x4 -> x0, waiting for transfers between devices: 351 us -> none  [the longest x1 110 us: local(): lax.all_gather(value_weight, 'fsdp', axis=0, tiled=True)]
    pallas_call x0 -> x1, Pallas kernels: none -> 88.4 us  [draft_plane(): pl.pallas_call(plane_kernel_body, out_shape=jax.ShapeDtypeStruct((8, 128)...]
    all_gather x2 -> x3, blocking collectives: 10.5 us -> 43.8 us  [the longest x1 33.1 us: pooled_summaries(): turned = lax.all_gather(turned, 'fsdp', axis=0)]
    dot_general x8 -> x5, matrix products: 37.1 us -> 8.76 us  [the longest x1 3.53 us: pooled_summaries(): jnp.dot(jnp.concatenate([high, low], axis=0), normed, preferred_element_t...]
    all_to_all x0 -> x2, starting transfers between devices: none -> 9.51 us  [the longest x1 5.83 us: pooled_summaries(): lax.all_to_all(pools, 'fsdp', 0, 0).reshape(groups * segs, KVH, depth)]
    unnamed x1 -> x0, blocking collectives: 6.34 us -> none
    all_to_all x0 -> x2, waiting for transfers between devices: none -> 5.02 us  [the longest x1 5.02 us: pooled_summaries(): lax.all_to_all(pools, 'fsdp', 0, 0).reshape(groups * segs, KVH, depth)]
  transfers between devices with their start and end apart: 4 -> 2, of which waited for: 4 -> 1; matrix products, arithmetic and copies ran while one was open for 9% -> 0% of each run, Pallas kernels for 0% -> 53%
where the time goes in v1:
time: 169 us; the launch traced here: 168 us
  Pallas kernels  88.4 us (52%)
  blocking collectives  43.8 us (26%)
  matrix products  9.9 us (6%)
  starting transfers between devices  9.51 us (6%)
  local copies, waits for them, and re-layouts  5.91 us (3%)
  waiting for transfers between devices  5.02 us (3%)
  other arithmetic  4.61 us (3%)
    pallas_call x1, Pallas kernels, draft_plane(): pl.pallas_call(plane_kernel_body, out_shape=jax.ShapeDtypeStruct((8, 128)...  88.4 us
    all_gather x1, blocking collectives, pooled_summaries(): turned = lax.all_gather(turned, 'fsdp', axis=0)  33.1 us
    all_to_all x1, starting transfers between devices, pooled_summaries(): lax.all_to_all(pools, 'fsdp', 0, 0).reshape(groups * segs, KVH, depth)  5.83 us
    all_gather x1, blocking collectives, local(): every = lax.all_gather(packed, 'seq', axis=0, tiled=True)  5.46 us
    all_gather x1, blocking collectives, draft_plane(): every = lax.all_gather(draft_head, 'seq', axis=0, tiled=True)  5.19 us
    all_to_all x1, waiting for transfers between devices, pooled_summaries(): lax.all_to_all(pools, 'fsdp', 0, 0).reshape(groups * segs, KVH, depth)  5.02 us
    all_to_all x1, starting transfers between devices, pooled_summaries(): partial = lax.all_to_all(partial.transpose(1, 0, 2, 3), 'fsdp', 0, 0)  3.68 us
    dot_general x1, matrix products, pooled_summaries(): jnp.dot(jnp.concatenate([high, low], axis=0), normed, preferred_element_t...  3.53 us
  transfers between devices with their start and end apart: 2, of which 1 were waited for; matrix products, arithmetic and copies ran while one was open for 0% of the time, Pallas kernels for 53%

profile of v1, /device:TPU:0, one launch (start us, length us, event | category | flops | bytes accessed | tf_op | source)
XLA Modules:
  0.0 168.1 jit_solution(5043883258142766999)
XLA Ops:
  0.6 0.0 copy-start
  0.7 1.2 copy-done
  1.9 1.6 fusion.9
  3.5 0.1 copy.45
  3.6 0.0 copy-start.4
  3.6 33.1 %all_gather.11 = f32[8,16,1024]{2,1,0:T(8,128)S(1)} all-gather(f32[1,16,1024]{2,1,0:T(8,128)S(1)} %div.70), channel_id=1, replica_groups=mesh['fsdp'=8,'seq'=4] {'fsdp'}, dimensions={0}, use_global_device_ids=true | all-gather | bytes 589824 | tf_op jit(solution)/shard_map/all_gather | solution.py:43
  36.8 0.1 reduce-precision_convert_fusion
  36.8 3.1 %fusion.2 = f32[256]{0:T(256)S(1)} fusion(bf16[256,8192]{1,0:T(8,128)(2,1)} %param.15), kind=kLoop, calls=%fused_computation.4 | loop fusion | flops 6291200 | bytes 4195328 | tf_op jit(solution)/shard_map/reduce_sum | solution.py:21
  40.0 0.0 copy-done.6
  40.0 0.0 copy-done.4
  40.0 1.4 fusion.7
  41.4 0.1 reshape.120
  41.5 0.0 copy-done.7
  41.5 0.1 select_reduce_fusion
  41.6 0.2 fusion.12
  41.8 0.1 broadcast_multiply_fusion
  41.9 0.1 mul.66
  42.0 3.5 %fusion.5 = f32[64,8192]{1,0:T(8,128)S(1)} fusion(bf16[256,8192]{1,0:T(8,128)(2,1)} %param.15, f32[8192]{0:T(1024)S(1)} %copy-done.6, f32[256]{0:T(256)S(1)} %add_rsqrt_fusion, bf16[32,256]{1,0:T(8,128)(2,1)S(1)} %get-tuple-element.11, bf16[32,256]{1,0:T(8,128)(2,1)S(1)} %get-tuple-element.10), kind=kOutput, calls=%fused_computation.7 | convolution fusion | flops 276889600 | bytes 6358016 | tf_op jit(solution)/shard_map/dot_general | solution.py:62
  45.5 0.0 copy-start.5
  45.5 0.1 fusion.25
  45.6 0.8 copy.93
  46.5 5.8 %all-to-all-start = ((bf16[8,32,1024]{2,1,0:T(8,128)(2,1)}), bf16[8,32,1024]{2,1,0:T(8,128)(2,1)S(1)}, u32[]{:S(2)}, u32[]{:S(2)}) async-start(bf16[8,32,1024]{2,1,0:T(8,128)(2,1)} %bitcast.87), calls=%async_computation | async-start | bytes 1048576 | tf_op jit(solution)/shard_map/all_to_all | solution.py:65
  52.3 0.0 copy-done.5
  52.3 5.2 %all_gather.10 = f32[4096]{0:T(1024)S(1)} all-gather(f32[1024]{0:T(1024)S(1)} %copy-done.5), channel_id=1, replica_groups=mesh['fsdp'=8,'seq'=4] {'seq'}, dimensions={0}, use_global_device_ids=true | all-gather | bytes 20480 | tf_op jit(solution)/shard_map/all_gather | solution.py:342
  57.5 0.1 dynamic_slice.3
  57.6 5.0 %all-to-all-done = bf16[8,32,1024]{2,1,0:T(8,128)(2,1)S(1)} async-done(((bf16[8,32,1024]{2,1,0:T(8,128)(2,1)}), bf16[8,32,1024]{2,1,0:T(8,128)(2,1)S(1)}, u32[]{:S(2)}, u32[]{:S(2)}) %all-to-all-start) | async-done | bytes 524320 | tf_op jit(solution)/shard_map/all_to_all | solution.py:65
  62.6 0.2 reshape.122
  62.8 0.5 convolution_bitcast_fusion.1
  63.3 1.7 %convolution_bitcast_fusion = f32[64,4,128]{2,0,1:T(8,128)S(1)} fusion(bf16[64,4,1024]{2,1,0:T(4,128)(2,1)S(1)} %reshape.122, bf16[1024,512]{1,0:T(8,128)(2,1)} %param.18), kind=kOutput, calls=%fused_computation.9 | convolution fusion | flops 67108864 | bytes 1703936 | tf_op jit(solution)/shard_map/ghd,dhk->ghk/dot_general | solution.py:68
  65.0 0.1 copy.54
  65.1 0.1 stack.10
  65.2 0.1 copy.51
  65.2 0.1 stack.9
  65.3 0.7 copy.55
  66.0 3.7 %all-to-all-start.1 = ((f32[8,2,8,512]{3,2,1,0:T(8,128)}), f32[8,2,8,512]{3,2,1,0:T(8,128)S(1)}, u32[]{:S(2)}, u32[]{:S(2)}) async-start(f32[8,2,8,512]{3,2,1,0:T(8,128)} %copy.55), calls=%async_computation.1 | async-start | bytes 524288 | tf_op jit(solution)/shard_map/all_to_all | solution.py:72
  69.7 0.0 copy-done.2
  69.7 0.0 copy-start.1
  69.8 2.2 %copy-done.1 = bf16[1024,2048]{1,0:T(8,128)(2,1)S(1)} copy-done((bf16[1024,2048]{1,0:T(8,128)(2,1)S(1)}, bf16[1024,2048]{1,0:T(8,128)(2,1)}, u32[]{:S(2)}) %copy-start.1) | copy-done | bytes 4194328
  71.9 88.4 %shard_map.122 = f32[8,128]{1,0:T(8,128)S(1)} custom-call(bf16[1024,2048]{1,0:T(8,128)(2,1)S(1)} %copy-done.1, bf16[256,1024]{1,0:T(8,128)(2,1)S(1)} %copy-done.2, bf16[256,1024]{1,0:T(8,128)(2,1)S(1)} %copy-done.3, f32[1,512]{1,0:T(1,128)S(1)} %bitcast.88), custom_call_target="tpu_custom_call" | custom-call | flops 8589934592 | bytes 25165824 | tf_op jit(solution)/shard_map/pallas_call | solution.py:345
  160.4 0.1 reduce_sum.54
  160.5 0.5 add_divide_fusion
  161.0 0.0 all-to-all-done.1
  161.1 0.1 broadcast_in_dim.72
  161.2 5.5 %all_gather.12 = f32[32,1152]{1,0:T(8,128)S(1)} all-gather(f32[8,1152]{1,0:T(8,128)S(1)} %pad_maximum_fusion), channel_id=1, replica_groups=mesh['fsdp'=8,'seq'=4] {'seq'}, dimensions={0}, use_global_device_ids=true | all-gather | bytes 184320 | tf_op jit(solution)/shard_map/all_gather | solution.py:412
  166.6 0.1 fusion.43
  166.7 0.3 fusion.54
  167.0 0.2 fusion.45
  167.2 0.9 fusion.20
  (22 shorter events, 0.2 us)
Async XLA Ops:
  0.6 1.2 copy-start
  1.9 38.1 %copy-start.6 = (f32[8192]{0:T(1024)S(1)}, f32[8192]{0:T(1024)}, u32[]{:S(2)}) copy-start(f32[8192]{0:T(1024)} %param.16) | copy-start | bytes 98308
  3.6 36.4 %copy-start.4 = (bf16[256,8192]{1,0:T(8,128)(2,1)S(1)}, bf16[256,8192]{1,0:T(8,128)(2,1)}, u32[]{:S(2)}) copy-start(bf16[256,8192]{1,0:T(8,128)(2,1)} %param.15) | copy-start | bytes 12582916
  39.9 1.6 copy-start.7
  45.5 6.8 %copy-start.5 = (f32[1024]{0:T(1024)S(1)}, f32[1024]{0:T(1024)}, u32[]{:S(2)}) copy-start(f32[1024]{0:T(1024)} %param.14) | copy-start | bytes 12292
  46.5 23.3 %copy-start.2 = (bf16[256,1024]{1,0:T(8,128)(2,1)S(1)}, bf16[256,1024]{1,0:T(8,128)(2,1)}, u32[]{:S(2)}) copy-start(bf16[256,1024]{1,0:T(8,128)(2,1)} %gate_hbm.1) | copy-start | bytes 1572868
  46.5 23.3 %copy-start.3 = (bf16[256,1024]{1,0:T(8,128)(2,1)S(1)}, bf16[256,1024]{1,0:T(8,128)(2,1)}, u32[]{:S(2)}) copy-start(bf16[256,1024]{1,0:T(8,128)(2,1)} %up_hbm.1) | copy-start | bytes 1572868
  46.5 16.1 %all-to-all-start = ((bf16[8,32,1024]{2,1,0:T(8,128)(2,1)}), bf16[8,32,1024]{2,1,0:T(8,128)(2,1)S(1)}, u32[]{:S(2)}, u32[]{:S(2)}) async-start(bf16[8,32,1024]{2,1,0:T(8,128)(2,1)} %bitcast.87), calls=%async_computation | async-start | bytes 1048576 | tf_op jit(solution)/shard_map/all_to_all | solution.py:65
  66.0 95.0 %all-to-all-start.1 = ((f32[8,2,8,512]{3,2,1,0:T(8,128)}), f32[8,2,8,512]{3,2,1,0:T(8,128)S(1)}, u32[]{:S(2)}, u32[]{:S(2)}) async-start(f32[8,2,8,512]{3,2,1,0:T(8,128)} %copy.55), calls=%async_computation.1 | async-start | bytes 524288 | tf_op jit(solution)/shard_map/all_to_all | solution.py:72
  69.7 2.2 %copy-start.1 = (bf16[1024,2048]{1,0:T(8,128)(2,1)S(1)}, bf16[1024,2048]{1,0:T(8,128)(2,1)}, u32[]{:S(2)}) copy-start(bf16[1024,2048]{1,0:T(8,128)(2,1)} %tok_hbm.1) | copy-start | bytes 12582916
  71.9 88.4 %copy-start.8 = (s32[8]{0:T(128)S(1)}, s32[8]{0:T(128)}, u32[]{:S(2)}) copy-start(s32[8]{0:T(128)} %param.20) | copy-start | bytes 100

commit v2 on v1

--- a/solution.py
+++ b/solution.py
@@ -25,6 +25,16 @@
 def split_pair(values):
     high = lax.reduce_precision(values, 8, 7)
     return high.astype(jnp.bfloat16), (values - high).astype(jnp.bfloat16)
+
+
+def query_rows(key_weight, pool_query):
+    depth = key_weight.shape[0]
+    return jnp.einsum(
+        "chk,dhk->chd",
+        pool_query,
+        key_weight.reshape(depth, KVH, HD).astype(jnp.float32),
+        precision=lax.Precision.HIGHEST,
+    ).reshape(pool_query.shape[0] * KVH, depth) / math.sqrt(HD)
 
 
 def pooled_summaries(normed, key_weight, value_weight, pool_query, owner):
@@ -34,12 +44,7 @@
     depth = key_weight.shape[0]
     key_heads = key_weight.reshape(depth, KVH, HD)
     value_heads = value_weight.reshape(depth, KVH, HD)
-    turned = jnp.einsum(
-        "chk,dhk->chd",
-        pool_query,
-        key_heads.astype(jnp.float32),
-        precision=lax.Precision.HIGHEST,
-    ).reshape(lanes * KVH, depth) / math.sqrt(HD)
+    turned = query_rows(key_weight, pool_query)
     turned = lax.all_gather(turned, "fsdp", axis=0)
     turned = turned.transpose(1, 0, 2).reshape(lanes * KVH, groups * depth)
     both = lax.dot_general(
@@ -110,10 +115,12 @@
 
 
 def plane_kernel_body(
-    tok_hbm, gate_hbm, up_hbm, head_ref, out_ref,
-    tok, wg, wu, sums, gathered,
+    tok_hbm, gate_hbm, up_hbm, head_in, normed, turned, pick, live, kw, vw,
+    out_ref, every_ref,
+    tok, wg, wu, sums, gathered, head_ref, every_turned, out_pools, pools, parts, back, every,
     tok_sem, first_send, near_send, far_send, arrive,
     tok_send, tok_arrive, sum_send, sum_arrive,
+    head_send, head_arrive, col_send, col_arrive, seq_send, seq_arrive,
 ):
     f = lax.axis_index("fsdp")
     s = lax.axis_index("seq")
@@ -130,24 +137,131 @@
         for ds in range(4):
             if dy or ds:
                 peers.append((dy, ds, 2 * z + lax.rem(y + dy, 2), lax.rem(s + ds, 4)))
+    columns = [lax.rem(f + d, 8) for d in range(1, 8)]
     for _, _, pf, ps in peers:
         pl.semaphore_signal(barrier, inc=1, device_id=(pf, ps), device_id_type=mesh_id)
-
-    @pl.when(z > 0)
-    def _():
-        pl.semaphore_signal(barrier, inc=1, device_id=(f - 2, s), device_id_type=mesh_id)
-
-    @pl.when(z < DEPTHS - 1)
-    def _():
-        pl.semaphore_signal(barrier, inc=1, device_id=(f + 2, s), device_id_type=mesh_id)
-
-    @pl.when(jnp.logical_or(z == 0, z == DEPTHS - 1))
-    def _():
-        pl.semaphore_wait(barrier, 8)
-
-    @pl.when(jnp.logical_and(z > 0, z < DEPTHS - 1))
-    def _():
-        pl.semaphore_wait(barrier, 9)
+    for cf in columns:
+        @pl.when(cf // 2 != z)
+        def _():
+            pl.semaphore_signal(barrier, inc=1, device_id=(cf, s), device_id_type=mesh_id)
+
+    pl.semaphore_wait(barrier, 13)
+
+    def column_copy(kind, number, source, target):
+        return pltpu.make_async_remote_copy(
+            src_ref=source,
+            dst_ref=target,
+            send_sem=col_send.at[kind, number],
+            recv_sem=col_arrive.at[kind, number],
+            device_id=(columns[number], s),
+            device_id_type=mesh_id,
+        )
+
+    def turned_copy(number):
+        return column_copy(0, number, turned, every_turned.at[f])
+
+    def pools_copy(number):
+        return column_copy(1, number, out_pools.at[number], pools.at[f])
+
+    def parts_copy(number):
+        return column_copy(2, number, parts.at[columns[number]], back.at[f])
+
+    def seq_copy(number):
+        return pltpu.make_async_remote_copy(
+            src_ref=every.at[s],
+            dst_ref=every.at[s],
+            send_sem=seq_send.at[number],
+            recv_sem=seq_arrive.at[number],
+            device_id=(f, lax.rem(s + number + 1, 4)),
+            device_id_type=mesh_id,
+        )
+
+    def head_copy(half):
+        return pltpu.make_async_remote_copy(
+            src_ref=head_in.at[:, half * WIDE : (half + 1) * WIDE],
+            dst_ref=head_ref,
+            send_sem=head_send,
+            recv_sem=head_arrive,
+            device_id=(f, 2 * x + half),
+            device_id_type=mesh_id,
+        )
+
+    for half in range(2):
+        @pl.when(jnp.logical_and(c == y, c != half))
+        def _():
+            head_copy(half).start()
+
+        @pl.when(jnp.logical_and(c == y, c == half))
+        def _():
+            head_ref[...] = head_in[:, half * WIDE : (half + 1) * WIDE]
+
+    for number in range(7):
+        turned_copy(number).start()
+    every_turned[f] = turned[...]
+
+    segs = 8
+    reach = kw.shape[0]
+    width = KVH * HD
+
+    def send_pools():
+        for number in range(7):
+            turned_copy(number).wait_recv()
+        both = jnp.zeros((32, segs * SEGL), jnp.float32)
+        for j in range(8):
+            values = every_turned[j]
+            high = values.astype(jnp.bfloat16)
+            low = (values - high.astype(jnp.float32)).astype(jnp.bfloat16)
+            both = both + lax.dot_general(
+                jnp.concatenate([high, low], axis=0),
+                normed[:, j * reach : (j + 1) * reach],
+                (((1,), (1,)), ((), ())),
+                preferred_element_type=jnp.float32,
+            )
+        scores = (both[:16] + both[16:]) * pick[...]
+        scores = jnp.sum(scores.reshape(4, KVH, segs * SEGL), axis=0)
+        wide = jnp.concatenate(
+            [jnp.broadcast_to(scores[h : h + 1], (segs, segs * SEGL)) for h in range(KVH)],
+            axis=0,
+        )
+        row = lax.broadcasted_iota(jnp.int32, wide.shape, 0) % segs
+        inside = lax.broadcasted_iota(jnp.int32, wide.shape, 1) // SEGL == row
+        wide = jnp.where(inside, wide, -1e30)
+        shares = jnp.where(inside, jnp.exp(wide - jnp.max(wide, axis=1, keepdims=True)), 0.0)
+        shares = shares / jnp.sum(shares, axis=1, keepdims=True)
+        high = shares.astype(jnp.bfloat16)
+        low = (shares - high.astype(jnp.float32)).astype(jnp.bfloat16)
+        pair = jnp.concatenate([high, low], axis=0)
+
+        def pool(j):
+            block = normed[:, pl.ds(pl.multiple_of(j * reach, reach), reach)]
+            result = jnp.dot(pair, block, preferred_element_type=jnp.float32)
+            return (result[:32] + result[32:]).astype(jnp.bfloat16)
+
+        for number in range(7):
+            out_pools[number] = pool(columns[number])
+            pools_copy(number).start()
+        pools[f] = pool(f)
+
+    def send_parts():
+        for number in range(7):
+            pools_copy(number).wait_recv()
+        block = pools[...].reshape(8 * 32, reach)
+        for which, ref in enumerate((kw, vw)):
+            result = jnp.dot(block, ref[...], preferred_element_type=jnp.float32)
+            result = result.reshape(8, KVH, segs, width)
+            for h in range(KVH):
+                start = which * width + h * HD
+                parts[:, :, start : start + HD] = result[:, h, :, h * HD : (h + 1) * HD]
+        for number in range(7):
+            parts_copy(number).start()
+        back[f] = parts[f]
+
+    def send_summaries():
+        for number in range(7):
+            parts_copy(number).wait_recv()
+        every[s] = jnp.concatenate([jnp.sum(back[...], axis=0), live[...]], axis=1)
+        for number in range(3):
+            seq_copy(number).start()
 
     def slot(ref, index):
         return ref.at[pl.ds(pl.multiple_of(index * depth, depth), depth), :]
@@ -278,6 +392,12 @@
     passed = 0
     for number, (distance, flip) in enumerate(order):
         turn(distance, flip, False)
+        if number == 1:
+            send_pools()
+        if number == 3:
+            send_parts()
+        if number == 5:
+            send_summaries()
         if number >= 2 and passed < chunks:
             tok_across(passed).wait_recv()
             tok_over(passed).start()
@@ -288,7 +408,12 @@
 
     tile = 512
     per = rows // 4
-    head = head_ref[...]
+
+    @pl.when(c != y)
+    def _():
+        head_copy(0).wait_recv()
+
+    head = head_ref[0:1, :]
 
     @pl.loop(0, 2 * rows // tile)
     def _(step):
@@ -320,6 +445,19 @@
         sum_copy(number, dy, pf, ps).wait_recv()
         total = total + gathered[number]
     out_ref[...] = total
+    for number in range(3):
+        seq_copy(number).wait_recv()
+    every_ref[...] = every[...]
+    for number in range(7):
+        turned_copy(number).wait_send()
+        pools_copy(number).wait_send()
+        parts_copy(number).wait_send()
+    for number in range(3):
+        seq_copy(number).wait_send()
+
+    @pl.when(c == y)
+    def _():
+        head_copy(0).wait_send()
 
     for half in range(2):
         @pl.when(jnp.logical_not(is_self(half)))
@@ -335,25 +473,43 @@
         sum_copy(number, dy, pf, ps).wait_send()
 
 
-def draft_plane(draft_tokens, draft_gate, draft_up, draft_head):
+def plane(
+    draft_tokens, draft_gate, draft_up, draft_head, normed, key_weight, value_weight,
+    pool_query, flags, owner,
+):
     rows, width = draft_tokens.shape
-    y = lax.axis_index("fsdp") % 2
-    x, c = lax.axis_index("seq") // 2, lax.axis_index("seq") % 2
-    every = lax.all_gather(draft_head, "seq", axis=0, tiled=True)
-    head = lax.dynamic_slice(every, ((2 * x + y) * 2 * WIDE + c * WIDE,), (WIDE,))
+    segs = flags.shape[0]
+    lanes = pool_query.shape[0]
+    depth = key_weight.shape[0]
+    turned = query_rows(key_weight, pool_query)
+    pick = (jnp.repeat(owner, SEGL)[None, :] == jnp.arange(lanes, dtype=jnp.int32)[:, None])
+    pick = jnp.repeat(pick.astype(jnp.float32), KVH, axis=0)
+    live = jnp.broadcast_to(flags.astype(jnp.float32)[:, None], (segs, 128))
+    head = jnp.broadcast_to(draft_head[None, :], (8, draft_head.shape[0]))
+    packed = 2 * KVH * HD + 128
     sems = pltpu.SemaphoreType.DMA
-    tiles = pl.pallas_call(
+    tiles, every = pl.pallas_call(
         plane_kernel_body,
-        out_shape=jax.ShapeDtypeStruct((8, 128), jnp.float32),
+        out_shape=(
+            jax.ShapeDtypeStruct((8, 128), jnp.float32),
+            jax.ShapeDtypeStruct((4, segs, packed), jnp.float32),
+        ),
         in_specs=[pl.BlockSpec(memory_space=pl.ANY)] * 3
-        + [pl.BlockSpec(memory_space=pltpu.VMEM)],
-        out_specs=pl.BlockSpec(memory_space=pltpu.VMEM),
+        + [pl.BlockSpec(memory_space=pltpu.VMEM)] * 7,
+        out_specs=(pl.BlockSpec(memory_space=pltpu.VMEM),) * 2,
         scratch_shapes=[
             pltpu.VMEM((2 * rows, width), jnp.bfloat16),
             pltpu.VMEM((width, WIDE), jnp.bfloat16),
             pltpu.VMEM((width, WIDE), jnp.bfloat16),
             pltpu.VMEM((8, 8, 128), jnp.float32),
             pltpu.VMEM((7, 8, 128), jnp.float32),
+            pltpu.VMEM((8, WIDE), jnp.float32),
+            pltpu.VMEM((8, lanes * KVH, depth), jnp.float32),
+            pltpu.VMEM((7, KVH * segs, depth), jnp.bfloat16),
+            pltpu.VMEM((8, KVH * segs, depth), jnp.bfloat16),
+            pltpu.VMEM((8, segs, packed - 128), jnp.float32),
+            pltpu.VMEM((8, segs, packed - 128), jnp.float32),
+            pltpu.VMEM((4, segs, packed), jnp.float32),
             sems,
             sems((2, 2)),
             sems((8, 2)),
@@ -363,17 +519,26 @@
             sems((2, 4)),
             sems((7,)),
             sems((7,)),
+            sems,
+            sems,
+            sems((3, 7)),
+            sems((3, 7)),
+            sems((3,)),
+            sems((3,)),
         ],
         compiler_params=pltpu.CompilerParams(
-            collective_id=0, has_side_effects=True, vmem_limit_bytes=40 * 1024 * 1024
+            collective_id=0, has_side_effects=True, vmem_limit_bytes=48 * 1024 * 1024
         ),
         cost_estimate=pl.CostEstimate(
             flops=4 * 2 * rows * width * WIDE,
             bytes_accessed=24 * 1024 * 1024,
             transcendentals=2 * rows * WIDE,
         ),
-    )(draft_tokens, draft_gate, draft_up, head[None, :])
-    return jnp.sum(tiles, axis=1) / SEGL
+    )(
+        draft_tokens, draft_gate, draft_up, head, normed, turned, pick, live,
+        key_weight, value_weight,
+    )
+    return jnp.sum(tiles, axis=1) / SEGL, every
 
 
 def local(
@@ -391,25 +556,30 @@
     owner,
 ):
     seg_count = flags.shape[0]
+    normed = normalize_rows(verifier_rows, norm_gain)
+    width = KVH * HD
     if plane_kernel:
-        draft_score = draft_plane(draft_tokens, draft_gate, draft_up, draft_head)
+        draft_score, every = plane(
+            draft_tokens, draft_gate, draft_up, draft_head, normed, key_weight, value_weight,
+            pool_query, flags, owner,
+        )
+        own = every[lax.axis_index("seq")]
+        summary_key = own[:, :width].reshape(seg_count, KVH, HD)
+        every = every.reshape(4 * seg_count, 2 * width + 128)
     else:
         draft_score = draft_gathered(draft_tokens, draft_gate, draft_up, draft_head, seg_count)
-    normed = normalize_rows(verifier_rows, norm_gain)
-    summary_key, summary_value = pooled_summaries(
-        normed, key_weight, value_weight, pool_query, owner
-    )
-    live_own = flags.astype(jnp.float32)
-    width = KVH * HD
-    packed = jnp.concatenate(
-        [
-            summary_key.reshape(seg_count, width),
-            summary_value.reshape(seg_count, width),
-            jnp.broadcast_to(live_own[:, None], (seg_count, 128)),
-        ],
-        axis=1,
-    )
-    every = lax.all_gather(packed, "seq", axis=0, tiled=True)
+        summary_key, summary_value = pooled_summaries(
+            normed, key_weight, value_weight, pool_query, owner
+        )
+        packed = jnp.concatenate(
+            [
+                summary_key.reshape(seg_count, width),
+                summary_value.reshape(seg_count, width),
+                jnp.broadcast_to(flags.astype(jnp.float32)[:, None], (seg_count, 128)),
+            ],
+            axis=1,
+        )
+        every = lax.all_gather(packed, "seq", axis=0, tiled=True)
     pooled = cross_pool(
         summary_key,
         every[:, :width].reshape(-1, KVH, HD),

time: 169 us -> 127 us (0.75)
  blocking collectives: 43.8 us -> 0 us
  Pallas kernels: 88.4 us -> 115 us
  starting transfers between devices: 9.51 us -> 0 us
  matrix products: 9.9 us -> 2.05 us
  waiting for transfers between devices: 5.02 us -> 0 us
  local copies, waits for them, and re-layouts: 5.91 us -> 1.24 us
  other arithmetic: 4.61 us -> 7.6 us
    all_gather x3 -> x0, blocking collectives: 43.8 us -> none  [the longest x1 33.1 us: pooled_summaries(): turned = lax.all_gather(turned, 'fsdp', axis=0)]
    pallas_call x1, Pallas kernels: 88.4 us -> 115 us  [plane(): pl.pallas_call(plane_kernel_body, out_shape=(jax.ShapeDtypeStruct((8, 128...]
    all_to_all x2 -> x0, starting transfers between devices: 9.51 us -> none  [the longest x1 5.83 us: pooled_summaries(): lax.all_to_all(pools, 'fsdp', 0, 0).reshape(groups * segs, KVH, depth)]
    dot_general x5 -> x1, matrix products: 8.76 us -> 0.91 us  [query_rows(): jnp.einsum('chk,dhk->chd', pool_query, key_weight.reshape(depth, KVH, HD)...]
    all_to_all x2 -> x0, waiting for transfers between devices: 5.02 us -> none  [the longest x1 5.02 us: pooled_summaries(): lax.all_to_all(pools, 'fsdp', 0, 0).reshape(groups * segs, KVH, depth)]
    unnamed x19, local copies, waits for them, and re-layouts: 3.44 us -> 0.07 us
    convert_element_type x5 -> x3, other arithmetic: 0.18 us -> 3.12 us  [the longest x1 3.11 us: normalize_rows(): return (values * scale * norm_gain).astype(jnp.bfloat16)]
  transfers between devices with their start and end apart: 2 -> 0, of which waited for: 1 -> 0; matrix products, arithmetic and copies ran while one was open for 0% -> 0% of each run, Pallas kernels for 53% -> 0%
where the time goes in v2:
time: 127 us
  Pallas kernels  115 us (91%)
  other arithmetic  7.6 us (6%)
  matrix products  2.05 us (2%)
    pallas_call x1, Pallas kernels, plane(): pl.pallas_call(plane_kernel_body, out_shape=(jax.ShapeDtypeStruct((8, 128...  115 us
    reduce_sum x1, other arithmetic, normalize_rows(): scale = lax.rsqrt(jnp.mean(values * values, axis=-1, keepdims=True) + eps)  3.54 us
    convert_element_type x1, other arithmetic, normalize_rows(): return (values * scale * norm_gain).astype(jnp.bfloat16)  3.11 us

profile of v2, /device:TPU:0, one launch (start us, length us, event | category | flops | bytes accessed | tf_op | source)
XLA Modules:
  0.0 127.0 jit_solution(11849404026018928985)
XLA Ops:
  0.6 0.0 copy-start
  0.6 0.0 copy-start.5
  0.7 0.0 copy-start.6
  0.7 0.8 broadcast_in_dim.59.head_in
  1.5 3.5 %fusion = f32[256]{0:T(256)S(1)} fusion(bf16[256,8192]{1,0:T(8,128)(2,1)} %param.15), kind=kLoop, calls=%fused_computation.2 | loop fusion | flops 6291200 | bytes 4195328 | tf_op jit(solution)/shard_map/reduce_sum | solution.py:21
  5.1 0.0 copy-done.5
  5.1 0.0 copy-done.6
  5.1 0.0 copy-start.1
  5.1 0.0 copy-start.7
  5.1 0.0 copy-start.8
  5.1 0.0 copy-start.2
  5.1 0.0 copy-start.3
  5.1 0.0 copy-start.4
  5.1 3.1 %fusion.2.normed = bf16[256,8192]{1,0:T(8,128)(2,1)} fusion(bf16[256,8192]{1,0:T(8,128)(2,1)S(1)} %copy-done.5, f32[8192]{0:T(1024)S(1)} %copy-done.6, f32[256]{0:T(256)S(1)} %add_rsqrt_fusion), kind=kLoop, calls=%fused_computation.4 | loop fusion | flops 8388608 | bytes 8422400 | tf_op jit(solution)/shard_map/convert_element_type | solution.py:22
  8.3 0.0 copy-done
  8.3 0.0 copy-done.1
  8.3 0.9 fusion.3
  9.2 0.1 copy.24
  9.3 0.0 copy-done.7
  9.3 0.1 broadcast_in_dim.60
  9.3 0.1 eq.19
  9.5 0.0 copy-done.8
  9.5 0.1 broadcast_in_dim.62.live
  9.5 0.0 copy-done.2
  9.6 0.0 copy-done.3
  9.6 0.0 copy-done.4
  9.6 115.4 %shard_map.122 = (f32[8,128]{1,0:T(8,128)S(1)}, f32[4,8,1152]{2,1,0:T(8,128)S(1)}) custom-call(bf16[1024,2048]{1,0:T(8,128)(2,1)} %tok_hbm.1, bf16[256,1024]{1,0:T(8,128)(2,1)S(1)} %copy-done.3, bf16[256,1024]{1,0:T(8,128)(2,1)S(1)} %copy-done.4, f32[8,1024]{1,0:T(8,128)S(1)} %broadcast_in_dim.59.head_in, bf16[256,8192]{1,0:T(8,128)(2,1)} %fusion.2.normed, ...), custom_call_target="tpu_custom_call" | custom-call | flops 8589934592 | bytes 25165824 | tf_op jit(solution)/shard_map/pallas_call | solution.py:491
  124.9 0.1 reduce_sum.28
  125.0 0.5 add_divide_fusion
  125.6 0.1 fusion.17
  125.7 0.3 fusion.25
  126.0 0.2 fusion.18
  126.2 0.8 fusion.10
  (9 shorter events, 0.1 us)
Async XLA Ops:
  0.6 7.6 %copy-start = (f32[4,4,128]{2,1,0:T(4,128)S(1)}, f32[4,4,128]{2,1,0:T(4,128)}, u32[]{:S(2)}) copy-start(f32[4,4,128]{2,1,0:T(4,128)} %param.19) | copy-start | bytes 24580
  0.6 4.4 %copy-start.5 = (bf16[256,8192]{1,0:T(8,128)(2,1)S(1)}, bf16[256,8192]{1,0:T(8,128)(2,1)}, u32[]{:S(2)}) copy-start(bf16[256,8192]{1,0:T(8,128)(2,1)} %param.15) | copy-start | bytes 12582916
  0.7 4.4 %copy-start.6 = (f32[8192]{0:T(1024)S(1)}, f32[8192]{0:T(1024)}, u32[]{:S(2)}) copy-start(f32[8192]{0:T(1024)} %param.16) | copy-start | bytes 98308
  5.1 3.2 %copy-start.1 = (bf16[1024,512]{1,0:T(8,128)(2,1)S(1)}, bf16[1024,512]{1,0:T(8,128)(2,1)}, u32[]{:S(2)}) copy-start(bf16[1024,512]{1,0:T(8,128)(2,1)} %kw.1) | copy-start | bytes 3145732
  5.1 4.2 %copy-start.7 = (s32[8]{0:T(128)S(1)}, s32[8]{0:T(128)}, u32[]{:S(2)}) copy-start(s32[8]{0:T(128)} %param.21) | copy-start | bytes 100
  5.1 4.4 %copy-start.8 = (s32[8]{0:T(128)S(1)}, s32[8]{0:T(128)}, u32[]{:S(2)}) copy-start(s32[8]{0:T(128)} %param.20) | copy-start | bytes 100
  5.1 4.4 %copy-start.2 = (bf16[1024,512]{1,0:T(8,128)(2,1)S(1)}, bf16[1024,512]{1,0:T(8,128)(2,1)}, u32[]{:S(2)}) copy-start(bf16[1024,512]{1,0:T(8,128)(2,1)} %vw.1) | copy-start | bytes 3145732
  5.1 4.4 %copy-start.3 = (bf16[256,1024]{1,0:T(8,128)(2,1)S(1)}, bf16[256,1024]{1,0:T(8,128)(2,1)}, u32[]{:S(2)}) copy-start(bf16[256,1024]{1,0:T(8,128)(2,1)} %gate_hbm.1) | copy-start | bytes 1572868
  5.1 4.4 %copy-start.4 = (bf16[256,1024]{1,0:T(8,128)(2,1)S(1)}, bf16[256,1024]{1,0:T(8,128)(2,1)}, u32[]{:S(2)}) copy-start(bf16[256,1024]{1,0:T(8,128)(2,1)} %up_hbm.1) | copy-start | bytes 1572868

commit v3 on v2

--- a/solution.py
+++ b/solution.py
@@ -389,19 +389,14 @@
                 both(index, -1, wait)
 
     order = ((0, 0), (1, 0), (0, 1), (2, 0), (1, 1), (3, 0), (2, 1), (3, 1))
-    passed = 0
     for number, (distance, flip) in enumerate(order):
         turn(distance, flip, False)
         if number == 1:
             send_pools()
-        if number == 3:
-            send_parts()
-        if number == 5:
-            send_summaries()
-        if number >= 2 and passed < chunks:
-            tok_across(passed).wait_recv()
-            tok_over(passed).start()
-            passed += 1
+    for chunk in range(chunks):
+        tok_across(chunk).wait_recv()
+        tok_over(chunk).start()
+    send_parts()
     for chunk in range(chunks):
         tok_over(chunk).wait_recv()
     own_tokens.wait()
@@ -427,6 +422,8 @@
             lanes = lanes + by_seg[:, lane * 128 : (lane + 1) * 128]
         for piece in range(tile // per):
             sums[(tile // per) * step + piece] = lanes[piece * 8 : (piece + 1) * 8, :]
+
+    send_summaries()
 
     def sum_copy(number, dy, pf, ps):
         return pltpu.make_async_remote_copy(

time: 127 us -> 130 us (1.024)
  Pallas kernels: 115 us -> 118 us
    pallas_call x1, Pallas kernels: 115 us -> 118 us  [plane(): pl.pallas_call(plane_kernel_body, out_shape=(jax.ShapeDtypeStruct((8, 128...]
where the time goes in v3:
time: 130 us
  Pallas kernels  118 us (91%)
  other arithmetic  7.6 us (6%)
  matrix products  2.05 us (2%)
    pallas_call x1, Pallas kernels, plane(): pl.pallas_call(plane_kernel_body, out_shape=(jax.ShapeDtypeStruct((8, 128...  118 us
    reduce_sum x1, other arithmetic, normalize_rows(): scale = lax.rsqrt(jnp.mean(values * values, axis=-1, keepdims=True) + eps)  3.54 us
    convert_element_type x1, other arithmetic, normalize_rows(): return (values * scale * norm_gain).astype(jnp.bfloat16)  3.11 us

profile of v3, /device:TPU:0, one launch (start us, length us, event | category | flops | bytes accessed | tf_op | source)
XLA Modules:
  0.0 129.5 jit_solution(14791703636867632274)
XLA Ops:
  0.6 0.0 copy-start
  0.6 0.0 copy-start.5
  0.7 0.0 copy-start.6
  0.7 0.8 broadcast_in_dim.59.head_in
  1.5 3.5 %fusion = f32[256]{0:T(256)S(1)} fusion(bf16[256,8192]{1,0:T(8,128)(2,1)} %param.15), kind=kLoop, calls=%fused_computation.2 | loop fusion | flops 6291200 | bytes 4195328 | tf_op jit(solution)/shard_map/reduce_sum | solution.py:21
  5.1 0.0 copy-done.5
  5.1 0.0 copy-done.6
  5.1 0.0 copy-start.1
  5.1 0.0 copy-start.7
  5.1 0.0 copy-start.8
  5.1 0.0 copy-start.2
  5.1 0.0 copy-start.3
  5.1 0.0 copy-start.4
  5.1 3.1 %fusion.2.normed = bf16[256,8192]{1,0:T(8,128)(2,1)} fusion(bf16[256,8192]{1,0:T(8,128)(2,1)S(1)} %copy-done.5, f32[8192]{0:T(1024)S(1)} %copy-done.6, f32[256]{0:T(256)S(1)} %add_rsqrt_fusion), kind=kLoop, calls=%fused_computation.4 | loop fusion | flops 8388608 | bytes 8422400 | tf_op jit(solution)/shard_map/convert_element_type | solution.py:22
  8.3 0.0 copy-done
  8.3 0.0 copy-done.1
  8.3 0.9 fusion.3
  9.2 0.1 copy.24
  9.3 0.0 copy-done.7
  9.3 0.1 broadcast_in_dim.60
  9.3 0.1 eq.19
  9.5 0.0 copy-done.8
  9.5 0.1 broadcast_in_dim.62.live
  9.5 0.0 copy-done.2
  9.6 0.0 copy-done.3
  9.6 0.0 copy-done.4
  9.6 117.9 %shard_map.122 = (f32[8,128]{1,0:T(8,128)S(1)}, f32[4,8,1152]{2,1,0:T(8,128)S(1)}) custom-call(bf16[1024,2048]{1,0:T(8,128)(2,1)} %tok_hbm.1, bf16[256,1024]{1,0:T(8,128)(2,1)S(1)} %copy-done.3, bf16[256,1024]{1,0:T(8,128)(2,1)S(1)} %copy-done.4, f32[8,1024]{1,0:T(8,128)S(1)} %broadcast_in_dim.59.head_in, bf16[256,8192]{1,0:T(8,128)(2,1)} %fusion.2.normed, ...), custom_call_target="tpu_custom_call" | custom-call | flops 8589934592 | bytes 25165824 | tf_op jit(solution)/shard_map/pallas_call | solution.py:488
  127.4 0.1 reduce_sum.28
  127.5 0.5 add_divide_fusion
  128.1 0.1 fusion.17
  128.2 0.3 fusion.25
  128.5 0.2 fusion.18
  128.7 0.8 fusion.10
  (9 shorter events, 0.1 us)
Async XLA Ops:
  0.6 7.6 %copy-start = (f32[4,4,128]{2,1,0:T(4,128)S(1)}, f32[4,4,128]{2,1,0:T(4,128)}, u32[]{:S(2)}) copy-start(f32[4,4,128]{2,1,0:T(4,128)} %param.19) | copy-start | bytes 24580
  0.6 4.4 %copy-start.5 = (bf16[256,8192]{1,0:T(8,128)(2,1)S(1)}, bf16[256,8192]{1,0:T(8,128)(2,1)}, u32[]{:S(2)}) copy-start(bf16[256,8192]{1,0:T(8,128)(2,1)} %param.15) | copy-start | bytes 12582916
  0.7 4.4 %copy-start.6 = (f32[8192]{0:T(1024)S(1)}, f32[8192]{0:T(1024)}, u32[]{:S(2)}) copy-start(f32[8192]{0:T(1024)} %param.16) | copy-start | bytes 98308
  5.1 3.2 %copy-start.1 = (bf16[1024,512]{1,0:T(8,128)(2,1)S(1)}, bf16[1024,512]{1,0:T(8,128)(2,1)}, u32[]{:S(2)}) copy-start(bf16[1024,512]{1,0:T(8,128)(2,1)} %kw.1) | copy-start | bytes 3145732
  5.1 4.2 %copy-start.7 = (s32[8]{0:T(128)S(1)}, s32[8]{0:T(128)}, u32[]{:S(2)}) copy-start(s32[8]{0:T(128)} %param.21) | copy-start | bytes 100
  5.1 4.4 %copy-start.8 = (s32[8]{0:T(128)S(1)}, s32[8]{0:T(128)}, u32[]{:S(2)}) copy-start(s32[8]{0:T(128)} %param.20) | copy-start | bytes 100
  5.1 4.4 %copy-start.2 = (bf16[1024,512]{1,0:T(8,128)(2,1)S(1)}, bf16[1024,512]{1,0:T(8,128)(2,1)}, u32[]{:S(2)}) copy-start(bf16[1024,512]{1,0:T(8,128)(2,1)} %vw.1) | copy-start | bytes 3145732
  5.1 4.4 %copy-start.3 = (bf16[256,1024]{1,0:T(8,128)(2,1)S(1)}, bf16[256,1024]{1,0:T(8,128)(2,1)}, u32[]{:S(2)}) copy-start(bf16[256,1024]{1,0:T(8,128)(2,1)} %gate_hbm.1) | copy-start | bytes 1572868
  5.1 4.4 %copy-start.4 = (bf16[256,1024]{1,0:T(8,128)(2,1)S(1)}, bf16[256,1024]{1,0:T(8,128)(2,1)}, u32[]{:S(2)}) copy-start(bf16[256,1024]{1,0:T(8,128)(2,1)} %up_hbm.1) | copy-start | bytes 1572868

commit v4 on v3

--- a/solution.py
+++ b/solution.py
@@ -324,8 +324,6 @@
             device_id_type=mesh_id,
         )
 
-    for chunk in range(chunks):
-        tok_across(chunk).start()
     own_tokens = pltpu.make_async_copy(tok_hbm, tok.at[pl.ds(0, rows), :], tok_sem)
     own_tokens.start()
 
@@ -393,10 +391,15 @@
         turn(distance, flip, False)
         if number == 1:
             send_pools()
+            for chunk in range(chunks):
+                tok_across(chunk).start()
+        if number == 3:
+            send_parts()
+        if number == 5:
+            send_summaries()
     for chunk in range(chunks):
         tok_across(chunk).wait_recv()
         tok_over(chunk).start()
-    send_parts()
     for chunk in range(chunks):
         tok_over(chunk).wait_recv()
     own_tokens.wait()
@@ -422,8 +425,6 @@
             lanes = lanes + by_seg[:, lane * 128 : (lane + 1) * 128]
         for piece in range(tile // per):
             sums[(tile // per) * step + piece] = lanes[piece * 8 : (piece + 1) * 8, :]
-
-    send_summaries()
 
     def sum_copy(number, dy, pf, ps):
         return pltpu.make_async_remote_copy(

time: 130 us -> 131 us (level)
    pallas_call x1, Pallas kernels: 118 us -> 119 us  [plane(): pl.pallas_call(plane_kernel_body, out_shape=(jax.ShapeDtypeStruct((8, 128...]
where the time goes in v4:
time: 131 us
  Pallas kernels  119 us (91%)
  other arithmetic  7.6 us (6%)
  matrix products  2.05 us (2%)
    pallas_call x1, Pallas kernels, plane(): pl.pallas_call(plane_kernel_body, out_shape=(jax.ShapeDtypeStruct((8, 128...  119 us
    reduce_sum x1, other arithmetic, normalize_rows(): scale = lax.rsqrt(jnp.mean(values * values, axis=-1, keepdims=True) + eps)  3.54 us
    convert_element_type x1, other arithmetic, normalize_rows(): return (values * scale * norm_gain).astype(jnp.bfloat16)  3.11 us

profile of v4, /device:TPU:0, one launch (start us, length us, event | category | flops | bytes accessed | tf_op | source)
XLA Modules:
  0.0 131.0 jit_solution(7909955370008788488)
XLA Ops:
  0.6 0.0 copy-start
  0.6 0.0 copy-start.5
  0.7 0.0 copy-start.6
  0.7 0.8 broadcast_in_dim.59.head_in
  1.5 3.5 %fusion = f32[256]{0:T(256)S(1)} fusion(bf16[256,8192]{1,0:T(8,128)(2,1)} %param.15), kind=kLoop, calls=%fused_computation.2 | loop fusion | flops 6291200 | bytes 4195328 | tf_op jit(solution)/shard_map/reduce_sum | solution.py:21
  5.1 0.0 copy-done.5
  5.1 0.0 copy-done.6
  5.1 0.0 copy-start.1
  5.1 0.0 copy-start.7
  5.1 0.0 copy-start.8
  5.1 0.0 copy-start.2
  5.1 0.0 copy-start.3
  5.1 0.0 copy-start.4
  5.1 3.1 %fusion.2.normed = bf16[256,8192]{1,0:T(8,128)(2,1)} fusion(bf16[256,8192]{1,0:T(8,128)(2,1)S(1)} %copy-done.5, f32[8192]{0:T(1024)S(1)} %copy-done.6, f32[256]{0:T(256)S(1)} %add_rsqrt_fusion), kind=kLoop, calls=%fused_computation.4 | loop fusion | flops 8388608 | bytes 8422400 | tf_op jit(solution)/shard_map/convert_element_type | solution.py:22
  8.3 0.0 copy-done
  8.3 0.0 copy-done.1
  8.3 0.9 fusion.3
  9.2 0.1 copy.24
  9.3 0.0 copy-done.7
  9.3 0.1 broadcast_in_dim.60
  9.3 0.1 eq.19
  9.5 0.0 copy-done.8
  9.5 0.1 broadcast_in_dim.62.live
  9.5 0.0 copy-done.2
  9.6 0.0 copy-done.3
  9.6 0.0 copy-done.4
  9.6 119.3 %shard_map.122 = (f32[8,128]{1,0:T(8,128)S(1)}, f32[4,8,1152]{2,1,0:T(8,128)S(1)}) custom-call(bf16[1024,2048]{1,0:T(8,128)(2,1)} %tok_hbm.1, bf16[256,1024]{1,0:T(8,128)(2,1)S(1)} %copy-done.3, bf16[256,1024]{1,0:T(8,128)(2,1)S(1)} %copy-done.4, f32[8,1024]{1,0:T(8,128)S(1)} %broadcast_in_dim.59.head_in, bf16[256,8192]{1,0:T(8,128)(2,1)} %fusion.2.normed, ...), custom_call_target="tpu_custom_call" | custom-call | flops 8589934592 | bytes 25165824 | tf_op jit(solution)/shard_map/pallas_call | solution.py:489
  128.9 0.1 reduce_sum.28
  129.0 0.5 add_divide_fusion
  129.5 0.1 fusion.17
  129.7 0.3 fusion.25
  129.9 0.2 fusion.18
  130.1 0.8 fusion.10
  (9 shorter events, 0.1 us)
Async XLA Ops:
  0.6 7.6 %copy-start = (f32[4,4,128]{2,1,0:T(4,128)S(1)}, f32[4,4,128]{2,1,0:T(4,128)}, u32[]{:S(2)}) copy-start(f32[4,4,128]{2,1,0:T(4,128)} %param.19) | copy-start | bytes 24580
  0.6 4.4 %copy-start.5 = (bf16[256,8192]{1,0:T(8,128)(2,1)S(1)}, bf16[256,8192]{1,0:T(8,128)(2,1)}, u32[]{:S(2)}) copy-start(bf16[256,8192]{1,0:T(8,128)(2,1)} %param.15) | copy-start | bytes 12582916
  0.7 4.4 %copy-start.6 = (f32[8192]{0:T(1024)S(1)}, f32[8192]{0:T(1024)}, u32[]{:S(2)}) copy-start(f32[8192]{0:T(1024)} %param.16) | copy-start | bytes 98308
  5.1 3.2 %copy-start.1 = (bf16[1024,512]{1,0:T(8,128)(2,1)S(1)}, bf16[1024,512]{1,0:T(8,128)(2,1)}, u32[]{:S(2)}) copy-start(bf16[1024,512]{1,0:T(8,128)(2,1)} %kw.1) | copy-start | bytes 3145732
  5.1 4.2 %copy-start.7 = (s32[8]{0:T(128)S(1)}, s32[8]{0:T(128)}, u32[]{:S(2)}) copy-start(s32[8]{0:T(128)} %param.21) | copy-start | bytes 100
  5.1 4.4 %copy-start.8 = (s32[8]{0:T(128)S(1)}, s32[8]{0:T(128)}, u32[]{:S(2)}) copy-start(s32[8]{0:T(128)} %param.20) | copy-start | bytes 100
  5.1 4.4 %copy-start.2 = (bf16[1024,512]{1,0:T(8,128)(2,1)S(1)}, bf16[1024,512]{1,0:T(8,128)(2,1)}, u32[]{:S(2)}) copy-start(bf16[1024,512]{1,0:T(8,128)(2,1)} %vw.1) | copy-start | bytes 3145732
  5.1 4.4 %copy-start.3 = (bf16[256,1024]{1,0:T(8,128)(2,1)S(1)}, bf16[256,1024]{1,0:T(8,128)(2,1)}, u32[]{:S(2)}) copy-start(bf16[256,1024]{1,0:T(8,128)(2,1)} %gate_hbm.1) | copy-start | bytes 1572868
  5.1 4.4 %copy-start.4 = (bf16[256,1024]{1,0:T(8,128)(2,1)S(1)}, bf16[256,1024]{1,0:T(8,128)(2,1)}, u32[]{:S(2)}) copy-start(bf16[256,1024]{1,0:T(8,128)(2,1)} %up_hbm.1) | copy-start | bytes 1572868
